TPU v7x, 32 devices: a whole 2x2x4 slice. The times are simulated.
32 devices in a mesh: row: 8 (over y, x, core), col: 4 (over z).
Axes of the slice: x: 2, y: 2, z: 4, core: 2. Of those that a mesh axis runs over, the one named last changes fastest.
Arguments:
- x_blocks: bfloat16 [8, 4, 16, 128, 128], P('row', 'col'), may hold values from -0.8984375 to 0.8984375
- x_live: int32 [8, 4, 16], P('row', 'col'), may hold values 0 or 1
- pair_slots: int32 [8, 4, 4, 3, 192], P('row', 'col'), may hold values from 0 to 15
- pair_count: int32 [8, 4, 4], P('row', 'col'), may hold values from 15 to 192, as said below
Outputs:
- gram_blocks: float32 [8, 4, 16, 128, 128], P('row', 'col')
Inputs may be any that keep to these rules, and one draw needn't show every extreme that they name: `pair_count`: live pairs of a tile at a section; some tile has exactly 192 at its first section.
All inputs are finite; a program needn't handle non-finite values. No bound on the sum of `x_live` on one device may be relied on, other than what follows from the above.
Results may differ from a plain program's by a relative error of at most 0.0003.
Values may be sent and summed in bfloat16 or wider, within the bound.
No kernel may reach another device: no remote copies, remote signals or barrier semaphores. Data moves between devices by JAX's collectives and lax.ppermute only.
A program may use at most 64 MiB of HBM per device.

v0:
```python
import functools

import jax
import jax.numpy as jnp
from jax import lax
from jax.experimental import pallas as pl
from jax.experimental.pallas import tpu as pltpu
from jax.sharding import PartitionSpec as P

SECTIONS = 4
UNROLL = 26
AXES = ("row", "col")
ROWS_BY_ROWS = (((1,), (1,)), ((), ()))
VLIM = 12
KSPACE = pl.ANY
AHEAD = 'AB'
FIRST = 8
COST = 0.25
KS = ({0: (0, 1), 1: (0, 1), 2: (0, 1)}, {0: (2, 3), 1: (2, 3), 2: (2, 3)}, {3: (0, 1, 2, 3)})
AFTER = {'L2B': ('Y0C',), 'L3A': ('R3B',), 'L3B': ('R3A',), 'X2A': ('X1A', 'Y1B'), 'X2B': ('X1A', 'X1B', 'Y1A', 'Y1B'), 'Y0C': ('X0A',), 'Y2A': ('X1A', 'Y1A', 'Y1B'), 'Y2B': ('X1A', 'Y1B')}


def pair_codes(pair_slots, pair_count, slots):
    pairs = pair_slots.shape[2]
    place = lax.iota(jnp.int32, pairs)
    left, right, out = pair_slots[:, 0], pair_slots[:, 1], pair_slots[:, 2]
    live = place[None, :] < pair_count[:, None]
    same = (out[:, :, None] == out[:, None, :]) & live[:, :, None] & live[:, None, :]
    rank = jnp.sum((same & (place[None, :] < place[:, None])[None]).astype(jnp.int32), axis=2)
    slot_ids = lax.iota(jnp.int32, slots)
    held = jnp.sum(((out[:, :, None] == slot_ids) & live[:, :, None]).astype(jnp.int32), axis=1)
    entries = (held + 1) // 2
    before = (out[:, :, None] > slot_ids).astype(jnp.int32)
    entry = jnp.sum(before * entries[:, None, :], axis=2) + rank // 2
    first = rank % 2 == 0
    part = jnp.where(first, (left - slots) + right * 2**12 + out * 2**24, (left - slots) * 2**6 + right * 2**18)
    room = (pairs + slots) // 2
    room = (room + UNROLL - 1) // UNROLL * UNROLL
    here = (entry[:, None, :] == lax.iota(jnp.int32, room)[None, :, None]) & live[:, None, :]
    codes = slots + slots * 2**6 + jnp.sum(jnp.where(here, part[:, None, :], 0), axis=2)
    return codes, jnp.sum(entries, axis=1)


def product_kernel(cfg, codes, meta, *refs):
    sections, allowed, tiles, left_of, right_of, has_sum = cfg
    tasks = len(sections)
    sum_ref = refs[-5] if has_sum else None
    out, left_buf, right_buf, sems = refs[-4:]
    slots = out.shape[0]
    shift = meta[SECTIONS]

    def tile_of(section):
        return lax.rem(section + SECTIONS - shift, SECTIONS)

    def wanted(i):
        tile = tile_of(sections[0] + i)
        yes = [tile == t for t in allowed[0]]
        if len(set(allowed)) > 1:
            yes = [(i == k) & (tile == t) for k in range(tasks) for t in allowed[k]]
        return functools.reduce(lambda a, b: a | b, yes)

    def copies(i):
        tile = tile_of(sections[i])
        wants = wanted(i)
        found = []
        start = 0
        for piece, (ref, size) in enumerate(left_of[i]):
            to = left_buf.at[i, pl.ds(start, size)]
            found.append((wants, pltpu.make_async_copy(refs[ref], to, sems.at[i, 0, piece])))
            start += size
        for t, pieces in zip(tiles, right_of):
            if t not in allowed[i]:
                continue
            start = 0
            for piece, (flag, near, far, size) in enumerate(pieces):
                to = right_buf.at[i, pl.ds(start, size)]
                sem = sems.at[i, 1, piece]
                if near == far:
                    found.append((tile == t, pltpu.make_async_copy(refs[near], to, sem)))
                else:
                    held = meta[SECTIONS + 1 + flag] == 1
                    found.append(((tile == t) & held, pltpu.make_async_copy(refs[near], to, sem)))
                    found.append(((tile == t) & ~held, pltpu.make_async_copy(refs[far], to, sem)))
                start += size
        return found

    for i in range(tasks):
        for condition, copy in copies(i):
            pl.when(condition)(copy.start)
    if has_sum:
        sum_copy = pltpu.make_async_copy(sum_ref, out, sems.at[tasks, 0, 0])
        sum_copy.start()
    for i in range(tasks):
        left_buf[i, slots] = jnp.zeros(left_buf.shape[2:], left_buf.dtype)
    if not has_sum:
        out[...] = jnp.zeros_like(out)

    def arrived(i):
        for side, (buf, sizes) in enumerate(
            ((left_buf, [n for _, n in left_of[0]]), (right_buf, [n for *_, n in right_of[0]]))
        ):
            start = 0
            for piece, size in enumerate(sizes):
                there = buf.at[i, pl.ds(start, size)]
                pltpu.make_async_copy(there, there, sems.at[i, side, piece]).wait()
                start += size

    if has_sum:
        sum_copy.wait()

    def one_task(i, carry):
        section = sections[0] + i
        pl.when(wanted(i))(lambda: arrived(i))
        blocks = jnp.where(wanted(i), (meta[section] + UNROLL - 1) // UNROLL, 0)

        def one_block(block, carry):
            products = []
            for u in range(UNROLL):
                code = codes[section, block * UNROLL + u]
                left = [left_buf[i, (code >> k) & 63] for k in (0, 6)]
                right = [right_buf[i, (code >> k) & 63] for k in (12, 18)]
                products.append(
                    lax.dot_general(
                        jnp.concatenate(left, axis=1),
                        jnp.concatenate(right, axis=1),
                        ROWS_BY_ROWS,
                        preferred_element_type=jnp.float32,
                    )
                )
            for u in range(UNROLL):
                slot = codes[section, block * UNROLL + u] >> 24
                out[slot] += products[u]
            return carry

        return lax.fori_loop(0, blocks, one_block, carry)

    lax.fori_loop(0, tasks, one_task, 0)


def add_terms(codes, meta, left, right, running, stage, slots, side):
    sections, allowed = tuple(stage), tuple(stage.values())
    tiles = tuple(sorted({t for some in allowed for t in some}))
    tasks = len(sections)
    operands = []

    def place(value):
        for k, known in enumerate(operands):
            if known is value:
                return k
        operands.append(value)
        return len(operands) - 1

    left_of = tuple(tuple((place(v), v.shape[0]) for v in left[s]) for s in sections)
    right_of = tuple(tuple((f, place(u), place(v), u.shape[0]) for f, u, v in right[t]) for t in tiles)
    if running is not None:
        operands.append(running)
    work = tasks * 96 * 2 * side * side * 2 * side
    return pl.pallas_call(
        functools.partial(product_kernel, (sections, allowed, tiles, left_of, right_of, running is not None)),
        out_shape=jax.ShapeDtypeStruct((slots, side, side), jnp.float32),
        in_specs=[pl.BlockSpec(memory_space=pltpu.SMEM)] * 2 + [pl.BlockSpec(memory_space=KSPACE)] * len(operands),
        out_specs=pl.BlockSpec(memory_space=pltpu.VMEM),
        scratch_shapes=[
            pltpu.VMEM((tasks, slots + 1, side, side), jnp.bfloat16),
            pltpu.VMEM((tasks, slots, side, side), jnp.bfloat16),
            pltpu.SemaphoreType.DMA((tasks + 1, 2, 2)),
        ],
        compiler_params=pltpu.CompilerParams(vmem_limit_bytes=VLIM * 2**20),
        cost_estimate=pl.CostEstimate(flops=int(COST * work), bytes_accessed=4 * 2**20, transcendentals=0),
    )(codes, meta, *operands)


def body(x_blocks, x_live, pair_slots, pair_count):
    row_total = lax.axis_size("row")
    col_total = lax.axis_size("col")
    layers = row_total // col_total
    panel = lax.axis_index("row") // layers
    col = lax.axis_index("col")
    slots, side = x_blocks.shape[2], x_blocks.shape[3]
    half = slots // 2

    def place(p, w, z):
        return (p * layers + w) * col_total + z

    everyone = [(p, w, z) for p in range(col_total) for w in range(layers) for z in range(col_total)]

    def moved(value, source_of):
        pairs = []
        for p, w, z in everyone:
            if source_of(p, z) is not None:
                q, y = source_of(p, z)
                pairs.append((place(q, w, y), place(p, w, z)))
        return lax.ppermute(value, AXES, pairs)

    filtered = jnp.where(x_live[0, 0][:, None, None] != 0, x_blocks[0, 0], jnp.zeros((), x_blocks.dtype))
    codes, entries = pair_codes(pair_slots[0, 0], pair_count[0, 0], slots)

    if col_total != SECTIONS:
        left, right = [], []
        for s in range(SECTIONS):
            left.append([filtered if s == 0 else moved(filtered, lambda p, z: (p, (z + s) % col_total))])
            value = moved(filtered, lambda p, z: (z, (p + s) % col_total))
            right.append([(0, value, value)])
        meta = jnp.concatenate([entries, jnp.zeros((4,), jnp.int32)])
        everything = {s: tuple(range(SECTIONS)) for s in range(SECTIONS)}
        total = add_terms(codes, meta, left, right, None, everything, slots, side)
        return total[None, None]

    near_x = panel % 2 == col % 2
    near_y = panel // 2 == col // 2
    next_y = panel // 2 == (col + 1) % SECTIONS // 2
    shift = (col - panel) % SECTIONS
    meta = jnp.concatenate([entries, jnp.stack([shift, near_x.astype(jnp.int32), near_y.astype(jnp.int32), 0 * shift])])
    done = {}

    def hop(name, value, source_of):
        waits = AFTER.get(name, ())
        if waits:
            value = lax.optimization_barrier((value,) + tuple(done[n] for n in waits))[0]
        with jax.named_scope(name):
            done[name] = moved(value, source_of)
        return done[name]

    def in_plane(name, value, flip, offset, far=False):
        def source_of(p, z):
            q = (z + offset) % SECTIONS
            return (p ^ flip, z) if p ^ flip == q or (far and p ^ flip == q ^ (3 - flip)) else None

        return hop(name, value, source_of)

    def along(name, value, by):
        return hop(name, value, lambda p, z: (p, (z + by) % SECTIONS))

    near = {1: near_x, 2: near_y}

    def stage_kernel(name, before, stage):
        done[name] = add_terms(codes, meta, left, right, done.get(before), stage, slots, side)

    made = {"a0": filtered[:FIRST], "b0": filtered[FIRST:]}
    ops = {}

    def op(name, operand, source_of):
        ops[name] = (operand, source_of)

    def get(name):
        if name not in made:
            if name in ops:
                operand, source_of = ops[name]
                value = operand()
                waits = [get(w) for w in AFTER.get(name, ())]
                if waits:
                    value = lax.optimization_barrier((value, *waits))[0]
                with jax.named_scope(name):
                    made[name] = moved(value, source_of)
            else:
                made[name] = values[name]()
        return made[name]

    def x_hop(p, z):
        return p ^ 1, z

    def y_hop(p, z):
        return p ^ 2, z

    def next_col(p, z):
        return p, (z + 1) % SECTIONS

    def last_col(p, z):
        return p, (z - 1) % SECTIONS

    values = {}
    for t in range(SECTIONS):
        la, lb = ("a0", "b0") if t == 0 else (f"L{t}A", f"L{t}B")
        if t:
            pa, pb = ("a0", "b0") if t == 1 else (f"L{t - 1}A", f"L{t - 1}B")
            op(la, functools.partial(get, pa), next_col)
            op(lb, functools.partial(get, pb), next_col)
        if t < SECTIONS - 1 or "A" not in AHEAD:
            op(f"X{t}A", functools.partial(get, la), x_hop)
            values[f"S{t}A"] = lambda t=t, la=la: lax.select(near_x, get(la), get(f"X{t}A"))
            op(f"Y{t}A", functools.partial(get, f"S{t}A"), y_hop)
        if t < SECTIONS - 1 or "B" not in AHEAD:
            op(f"Y{t}B", functools.partial(get, lb), y_hop)
            values[f"S{t}B"] = lambda t=t, lb=lb: lax.select(near_y, get(lb), get(f"Y{t}B"))
            op(f"X{t}B", functools.partial(get, f"S{t}B"), x_hop)
    if AHEAD:
        values["S0C"] = lambda: lax.select(near_x, get("X0A"), get("a0"))
        values["S0D"] = lambda: lax.select(next_y, get("b0"), get("Y0B"))
        op("Y0C", functools.partial(get, "S0C"), y_hop)
        op("X0D", functools.partial(get, "S0D"), x_hop)
        values["F0C"] = lambda: lax.select(next_y, get("S0C"), get("Y0C"))
        values["F0D"] = lambda: lax.select(near_x, get("X0D"), get("S0D"))
        op("R3A", functools.partial(get, "F0C"), last_col)
        op("R3B", functools.partial(get, "F0D"), last_col)

    def left_of(s):
        return [get("a0"), get("b0")] if s == 0 else [get(f"L{s}A"), get(f"L{s}B")]

    def right_of(t):
        ahead = AHEAD if t == SECTIONS - 1 else ""
        a = (0, get("R3A"), get("R3A")) if "A" in ahead else (1, get(f"S{t}A"), get(f"Y{t}A"))
        b = (0, get("R3B"), get("R3B")) if "B" in ahead else (0, get(f"S{t}B"), get(f"X{t}B"))
        return [a, b]

    def kernel_stage(k):
        stage = KS[k]
        tiles = sorted({t for some in stage.values() for t in some})
        left, right = {s: left_of(s) for s in stage}, {t: right_of(t) for t in tiles}
        running = get(f"K{k - 1}") if k else None
        waits = [get(w) for w in AFTER.get(f"K{k}", ())]
        c = codes
        if waits:
            c = lax.optimization_barrier((codes, *waits))[0]
        return add_terms(c, meta, left, right, running, stage, slots, side)

    for k in range(len(KS)):
        values[f"K{k}"] = functools.partial(kernel_stage, k)
    done["K3"] = get(f"K{len(KS) - 1}")
    return done["K3"][None, None]


def solution(mesh):
    return jax.shard_map(
        body,
        mesh=mesh,
        in_specs=(
            P("row", "col", None, None, None),
            P("row", "col", None),
            P("row", "col", None, None, None),
            P("row", "col", None),
        ),
        out_specs=P("row", "col", None, None, None),
        check_vma=False,
    )
```

profile of v0, /device:TPU:2, one launch (start us, length us, event | category | flops | bytes accessed | tf_op | source)
XLA Modules:
  0.0 66.4 jit_solution(17411481121257651479)
XLA Ops:
  0.0 0.7 compare_bitcast_fusion
  0.7 1.1 %bitcast_select_fusion = bf16[16,128,128]{2,1,0:T(8,128)(2,1)S(1)} fusion(bf16[1,1,16,128,128]{4,3,2,1,0:T(8,128)(2,1)} %param.4, pred[16]{0:T(512)(128)(4,1)S(1)} %compare_bitcast_fusion), kind=kLoop, calls=%fused_computation.1 | loop fusion | flops 262144 | bytes 1048592 | tf_op jit(solution)/shard_map/jit(_where)/select_n | solution.py:195
  1.9 1.6 %collective-permute-start.2 = (bf16[8,128,128]{2,1,0:T(8,128)(2,1)S(1)}, bf16[8,128,128]{2,1,0:T(8,128)(2,1)S(1)}, u32[]{:S(2)}, u32[]{:S(2)}) collective-permute-start(bf16[8,128,128]{2,1,0:T(8,128)(2,1)S(1)} %get-tuple-element.29.refs_1_), channel_id=1, source_target_pairs={{16,0},{17,1},{18,2},{19,3},{20,4},{21,5},{22,6},{23,7},{24,8},{25... | collective-permute-start | bytes 786440 | tf_op jit(solution)/shard_map/Y0B/ppermute | solution.py:193
  3.4 3.6 %collective-permute-start.6 = (bf16[8,128,128]{2,1,0:T(8,128)(2,1)S(1)}, bf16[8,128,128]{2,1,0:T(8,128)(2,1)S(1)}, u32[]{:S(2)}, u32[]{:S(2)}) collective-permute-start(bf16[8,128,128]{2,1,0:T(8,128)(2,1)S(1)} %get-tuple-element.29.refs_1_), channel_id=1, source_target_pairs={{1,0},{2,1},{3,2},{0,3},{5,4},{6,5},{7,6},{4,7},{9,8},{10,9},{11,1... | collective-permute-start | bytes 786440 | tf_op jit(solution)/shard_map/L1B/ppermute | solution.py:193
  8.1 0.6 copy-done.1
  9.8 4.8 %collective-permute-done.7 = bf16[8,128,128]{2,1,0:T(8,128)(2,1)S(1)} collective-permute-done((bf16[8,128,128]{2,1,0:T(8,128)(2,1)S(1)}, bf16[8,128,128]{2,1,0:T(8,128)(2,1)S(1)}, u32[]{:S(2)}, u32[]{:S(2)}) %collective-permute-start.7) | collective-permute-done | bytes 262176 | tf_op jit(solution)/shard_map/X0A/ppermute | solution.py:193
  15.2 2.8 %collective-permute-done.refs_2_ = bf16[8,128,128]{2,1,0:T(8,128)(2,1)S(1)} collective-permute-done((bf16[8,128,128]{2,1,0:T(8,128)(2,1)S(1)}, bf16[8,128,128]{2,1,0:T(8,128)(2,1)S(1)}, u32[]{:S(2)}, u32[]{:S(2)}) %collective-permute-start) | collective-permute-done | bytes 262176 | tf_op jit(solution)/shard_map/L1A/ppermute | solution.py:193
  18.5 4.3 %collective-permute-start.1 = (bf16[8,128,128]{2,1,0:T(8,128)(2,1)S(1)}, bf16[8,128,128]{2,1,0:T(8,128)(2,1)S(1)}, u32[]{:S(2)}, u32[]{:S(2)}) collective-permute-start(bf16[8,128,128]{2,1,0:T(8,128)(2,1)S(1)} %collective-permute-done.refs_2_), channel_id=1, source_target_pairs={{1,0},{2,1},{3,2},{0,3},{5,4},{6,5},{7,6},{4,7},{9,8},{10,9},{11,1... | collective-permute-start | bytes 786440 | tf_op jit(solution)/shard_map/L2A/ppermute | solution.py:193
  23.9 1.5 %collective-permute-start.3 = (bf16[8,128,128]{2,1,0:T(8,128)(2,1)S(1)}, bf16[8,128,128]{2,1,0:T(8,128)(2,1)S(1)}, u32[]{:S(2)}, u32[]{:S(2)}) collective-permute-start(bf16[8,128,128]{2,1,0:T(8,128)(2,1)S(1)} %get-tuple-element.24), channel_id=1, source_target_pairs={{8,0},{9,1},{10,2},{11,3},{12,4},{13,5},{14,6},{15,7},{0,8},{1,9},... | collective-permute-start | bytes 786440 | tf_op jit(solution)/shard_map/X0D/ppermute | solution.py:193
  25.5 1.6 %collective-permute-start.15 = (bf16[8,128,128]{2,1,0:T(8,128)(2,1)S(1)}, bf16[8,128,128]{2,1,0:T(8,128)(2,1)S(1)}, u32[]{:S(2)}, u32[]{:S(2)}) collective-permute-start(bf16[8,128,128]{2,1,0:T(8,128)(2,1)S(1)} %broadcast_select_fusion.6.refs_10_.refs_6_), channel_id=1, source_target_pairs={{16,0},{17,1},{18,2},{19,3},{20,4},{21,5},{22,6},{23,7},{24,8},{25... | collective-permute-start | bytes 786440 | tf_op jit(solution)/shard_map/Y1A/ppermute | solution.py:193
  27.1 4.8 %collective-permute-done.16 = bf16[8,128,128]{2,1,0:T(8,128)(2,1)S(1)} collective-permute-done((bf16[8,128,128]{2,1,0:T(8,128)(2,1)S(1)}, bf16[8,128,128]{2,1,0:T(8,128)(2,1)S(1)}, u32[]{:S(2)}, u32[]{:S(2)}) %collective-permute-start.16) | collective-permute-done | bytes 262176 | tf_op jit(solution)/shard_map/Y1B/ppermute | solution.py:193
  31.9 1.5 %collective-permute-start.18 = (bf16[8,128,128]{2,1,0:T(8,128)(2,1)S(1)}, bf16[8,128,128]{2,1,0:T(8,128)(2,1)S(1)}, u32[]{:S(2)}, u32[]{:S(2)}) collective-permute-start(bf16[8,128,128]{2,1,0:T(8,128)(2,1)S(1)} %collective-permute-done.1.refs_4_), channel_id=1, source_target_pairs={{8,0},{9,1},{10,2},{11,3},{12,4},{13,5},{14,6},{15,7},{0,8},{1,9},... | collective-permute-start | bytes 786440 | tf_op jit(solution)/shard_map/X2A/ppermute | solution.py:193
  33.6 1.6 %collective-permute-done.9.refs_5_ = bf16[8,128,128]{2,1,0:T(8,128)(2,1)S(1)} collective-permute-done((bf16[8,128,128]{2,1,0:T(8,128)(2,1)S(1)}, bf16[8,128,128]{2,1,0:T(8,128)(2,1)S(1)}, u32[]{:S(2)}, u32[]{:S(2)}) %collective-permute-start.9) | collective-permute-done | bytes 262176 | tf_op jit(solution)/shard_map/L2B/ppermute | solution.py:193
  35.6 1.2 %collective-permute-done.15.refs_11_.refs_7_ = bf16[8,128,128]{2,1,0:T(8,128)(2,1)S(1)} collective-permute-done((bf16[8,128,128]{2,1,0:T(8,128)(2,1)S(1)}, bf16[8,128,128]{2,1,0:T(8,128)(2,1)S(1)}, u32[]{:S(2)}, u32[]{:S(2)}) %collective-permute-start.15) | collective-permute-done | bytes 262176 | tf_op jit(solution)/shard_map/Y1A/ppermute | solution.py:193
  37.4 3.4 %collective-permute-done.18 = bf16[8,128,128]{2,1,0:T(8,128)(2,1)S(1)} collective-permute-done((bf16[8,128,128]{2,1,0:T(8,128)(2,1)S(1)}, bf16[8,128,128]{2,1,0:T(8,128)(2,1)S(1)}, u32[]{:S(2)}, u32[]{:S(2)}) %collective-permute-start.18) | collective-permute-done | bytes 262176 | tf_op jit(solution)/shard_map/X2A/ppermute | solution.py:193
  40.8 1.5 %collective-permute-start.17 = (bf16[8,128,128]{2,1,0:T(8,128)(2,1)S(1)}, bf16[8,128,128]{2,1,0:T(8,128)(2,1)S(1)}, u32[]{:S(2)}, u32[]{:S(2)}) collective-permute-start(bf16[8,128,128]{2,1,0:T(8,128)(2,1)S(1)} %broadcast_select_fusion.1.refs_12_.refs_8_), channel_id=1, source_target_pairs={{8,0},{9,1},{10,2},{11,3},{12,4},{13,5},{14,6},{15,7},{0,8},{1,9},... | collective-permute-start | bytes 786440 | tf_op jit(solution)/shard_map/X1B/ppermute | solution.py:193
  42.3 0.9 %collective-permute-start.13 = (bf16[8,128,128]{2,1,0:T(8,128)(2,1)S(1)}, bf16[8,128,128]{2,1,0:T(8,128)(2,1)S(1)}, u32[]{:S(2)}, u32[]{:S(2)}) collective-permute-start(bf16[8,128,128]{2,1,0:T(8,128)(2,1)S(1)} %get-tuple-element.23.refs_8_.refs_4_), channel_id=1, source_target_pairs={{8,0},{9,1},{10,2},{11,3},{12,4},{13,5},{14,6},{15,7},{0,8},{1,9},... | collective-permute-start | bytes 786440 | tf_op jit(solution)/shard_map/X0B/ppermute | solution.py:193
  43.2 1.3 %collective-permute-done.4.refs_11_.refs_15_ = bf16[8,128,128]{2,1,0:T(8,128)(2,1)S(1)} collective-permute-done((bf16[8,128,128]{2,1,0:T(8,128)(2,1)S(1)}, bf16[8,128,128]{2,1,0:T(8,128)(2,1)S(1)}, u32[]{:S(2)}, u32[]{:S(2)}) %collective-permute-start.4) | collective-permute-done | bytes 262176 | tf_op jit(solution)/shard_map/R3B/ppermute | solution.py:193
  45.0 3.6 %collective-permute-start.11 = (bf16[8,128,128]{2,1,0:T(8,128)(2,1)S(1)}, bf16[8,128,128]{2,1,0:T(8,128)(2,1)S(1)}, u32[]{:S(2)}, u32[]{:S(2)}) collective-permute-start(bf16[8,128,128]{2,1,0:T(8,128)(2,1)S(1)} %collective-permute-done.9.refs_5_), channel_id=1, source_target_pairs={{1,0},{2,1},{3,2},{0,3},{5,4},{6,5},{7,6},{4,7},{9,8},{10,9},{11,1... | collective-permute-start | bytes 786440 | tf_op jit(solution)/shard_map/L3B/ppermute | solution.py:193
  49.2 1.5 %collective-permute-start.21 = (bf16[8,128,128]{2,1,0:T(8,128)(2,1)S(1)}, bf16[8,128,128]{2,1,0:T(8,128)(2,1)S(1)}, u32[]{:S(2)}, u32[]{:S(2)}) collective-permute-start(bf16[8,128,128]{2,1,0:T(8,128)(2,1)S(1)} %broadcast_select_fusion.refs_8_.refs_12_), channel_id=1, source_target_pairs={{8,0},{9,1},{10,2},{11,3},{12,4},{13,5},{14,6},{15,7},{0,8},{1,9},... | collective-permute-start | bytes 786440 | tf_op jit(solution)/shard_map/X2B/ppermute | solution.py:193
  50.7 3.7 %shard_map.46.refs_12_ = f32[16,128,128]{2,1,0:T(8,128)S(1)} custom-call(s32[4,104]{1,0:T(4,128)S(1)} %broadcast_add_fusion.codes, s32[8]{0:T(128)S(1)} %concatenate.3.meta, bf16[8,128,128]{2,1,0:T(8,128)(2,1)S(1)} %get-tuple-element.30.refs_0_, bf16[8,128,128]{2,1,0:T(8,128)(2,1)S(1)} %get-tuple-element.29.refs_1_, ...), custom_call_target="tpu_custom_call" | custom-call | flops 603979776 | bytes 4194304 | tf_op jit(solution)/shard_map/pallas_call | solution.py:158
  54.5 1.1 %collective-permute-done.21.refs_9_.refs_13_ = bf16[8,128,128]{2,1,0:T(8,128)(2,1)S(1)} collective-permute-done((bf16[8,128,128]{2,1,0:T(8,128)(2,1)S(1)}, bf16[8,128,128]{2,1,0:T(8,128)(2,1)S(1)}, u32[]{:S(2)}, u32[]{:S(2)}) %collective-permute-start.21) | collective-permute-done | bytes 262176 | tf_op jit(solution)/shard_map/X2B/ppermute | solution.py:193
  55.6 6.4 %shard_map.47.refs_16_ = f32[16,128,128]{2,1,0:T(8,128)S(1)} custom-call(s32[4,104]{1,0:T(4,128)S(1)} %broadcast_add_fusion.codes, s32[8]{0:T(128)S(1)} %concatenate.3.meta, bf16[8,128,128]{2,1,0:T(8,128)(2,1)S(1)} %get-tuple-element.30.refs_0_, bf16[8,128,128]{2,1,0:T(8,128)(2,1)S(1)} %get-tuple-element.29.refs_1_, ...), custom_call_target="tpu_custom_call" | custom-call | flops 603979776 | bytes 4194304 | tf_op jit(solution)/shard_map/pallas_call | solution.py:158
  62.0 4.4 %shard_map.48 = f32[16,128,128]{2,1,0:T(8,128)} custom-call(s32[4,104]{1,0:T(4,128)S(1)} %broadcast_add_fusion.codes, s32[8]{0:T(128)S(1)} %concatenate.3.meta, bf16[8,128,128]{2,1,0:T(8,128)(2,1)S(1)} %collective-permute-done.5.refs_0_, bf16[8,128,128]{2,1,0:T(8,128)(2,1)S(1)} %collective-permute-done.11.refs_1_, ...), custom_call_target="tpu_custom_call" | custom-call | flops 201326592 | bytes 4194304 | tf_op jit(solution)/shard_map/pallas_call | solution.py:158
  (49 shorter events, 6.6 us)
Async XLA Ops:
  1.9 12.7 %collective-permute-start.2 = (bf16[8,128,128]{2,1,0:T(8,128)(2,1)S(1)}, bf16[8,128,128]{2,1,0:T(8,128)(2,1)S(1)}, u32[]{:S(2)}, u32[]{:S(2)}) collective-permute-start(bf16[8,128,128]{2,1,0:T(8,128)(2,1)S(1)} %get-tuple-element.29.refs_1_), channel_id=1, source_target_pairs={{16,0},{17,1},{18,2},{19,3},{20,4},{21,5},{22,6},{23,7},{24,8},{25... | collective-permute-start | bytes 786440 | tf_op jit(solution)/shard_map/Y0B/ppermute | solution.py:193
  3.4 19.4 %collective-permute-start.6 = (bf16[8,128,128]{2,1,0:T(8,128)(2,1)S(1)}, bf16[8,128,128]{2,1,0:T(8,128)(2,1)S(1)}, u32[]{:S(2)}, u32[]{:S(2)}) collective-permute-start(bf16[8,128,128]{2,1,0:T(8,128)(2,1)S(1)} %get-tuple-element.29.refs_1_), channel_id=1, source_target_pairs={{1,0},{2,1},{3,2},{0,3},{5,4},{6,5},{7,6},{4,7},{9,8},{10,9},{11,1... | collective-permute-start | bytes 786440 | tf_op jit(solution)/shard_map/L1B/ppermute | solution.py:193
  7.0 1.0 %copy-start = (s32[1,1,4,3,192]{4,2,3,1,0:T(4,128)S(1)}, s32[1,1,4,3,192]{4,2,3,1,0:T(4,128)}, u32[]{:S(2)}) copy-start(s32[1,1,4,3,192]{4,2,3,1,0:T(4,128)} %param.6) | copy-start | bytes 27652
  7.0 7.5 %collective-permute-start.7 = (bf16[8,128,128]{2,1,0:T(8,128)(2,1)S(1)}, bf16[8,128,128]{2,1,0:T(8,128)(2,1)S(1)}, u32[]{:S(2)}, u32[]{:S(2)}) collective-permute-start(bf16[8,128,128]{2,1,0:T(8,128)(2,1)S(1)} %get-tuple-element.30.refs_0_), channel_id=1, source_target_pairs={{8,0},{9,1},{10,2},{11,3},{12,4},{13,5},{14,6},{15,7},{0,8},{1,9},... | collective-permute-start | bytes 786440 | tf_op jit(solution)/shard_map/X0A/ppermute | solution.py:193
  7.6 10.4 %collective-permute-start = (bf16[8,128,128]{2,1,0:T(8,128)(2,1)S(1)}, bf16[8,128,128]{2,1,0:T(8,128)(2,1)S(1)}, u32[]{:S(2)}, u32[]{:S(2)}) collective-permute-start(bf16[8,128,128]{2,1,0:T(8,128)(2,1)S(1)} %get-tuple-element.30.refs_0_), channel_id=1, source_target_pairs={{1,0},{2,1},{3,2},{0,3},{5,4},{6,5},{7,6},{4,7},{9,8},{10,9},{11,1... | collective-permute-start | bytes 786440 | tf_op jit(solution)/shard_map/L1A/ppermute | solution.py:193
  8.1 0.7 copy-start.1
  14.6 10.8 %collective-permute-start.8 = (bf16[8,128,128]{2,1,0:T(8,128)(2,1)S(1)}, bf16[8,128,128]{2,1,0:T(8,128)(2,1)S(1)}, u32[]{:S(2)}, u32[]{:S(2)}) collective-permute-start(bf16[8,128,128]{2,1,0:T(8,128)(2,1)S(1)} %get-tuple-element.14), channel_id=1, source_target_pairs={{16,0},{17,1},{18,2},{19,3},{20,4},{21,5},{22,6},{23,7},{24,8},{25... | collective-permute-start | bytes 786440 | tf_op jit(solution)/shard_map/Y0C/ppermute | solution.py:193
  18.0 7.6 %collective-permute-start.14 = (bf16[8,128,128]{2,1,0:T(8,128)(2,1)S(1)}, bf16[8,128,128]{2,1,0:T(8,128)(2,1)S(1)}, u32[]{:S(2)}, u32[]{:S(2)}) collective-permute-start(bf16[8,128,128]{2,1,0:T(8,128)(2,1)S(1)} %collective-permute-done.refs_2_), channel_id=1, source_target_pairs={{8,0},{9,1},{10,2},{11,3},{12,4},{13,5},{14,6},{15,7},{0,8},{1,9},... | collective-permute-start | bytes 786440 | tf_op jit(solution)/shard_map/X1A/ppermute | solution.py:193
  18.5 13.4 %collective-permute-start.1 = (bf16[8,128,128]{2,1,0:T(8,128)(2,1)S(1)}, bf16[8,128,128]{2,1,0:T(8,128)(2,1)S(1)}, u32[]{:S(2)}, u32[]{:S(2)}) collective-permute-start(bf16[8,128,128]{2,1,0:T(8,128)(2,1)S(1)} %collective-permute-done.refs_2_), channel_id=1, source_target_pairs={{1,0},{2,1},{3,2},{0,3},{5,4},{6,5},{7,6},{4,7},{9,8},{10,9},{11,1... | collective-permute-start | bytes 786440 | tf_op jit(solution)/shard_map/L2A/ppermute | solution.py:193
  22.8 9.1 %collective-permute-start.16 = (bf16[8,128,128]{2,1,0:T(8,128)(2,1)S(1)}, bf16[8,128,128]{2,1,0:T(8,128)(2,1)S(1)}, u32[]{:S(2)}, u32[]{:S(2)}) collective-permute-start(bf16[8,128,128]{2,1,0:T(8,128)(2,1)S(1)} %collective-permute-done.6.refs_3_), channel_id=1, source_target_pairs={{16,0},{17,1},{18,2},{19,3},{20,4},{21,5},{22,6},{23,7},{24,8},{25... | collective-permute-start | bytes 786440 | tf_op jit(solution)/shard_map/Y1B/ppermute | solution.py:193
  23.9 9.6 %collective-permute-start.3 = (bf16[8,128,128]{2,1,0:T(8,128)(2,1)S(1)}, bf16[8,128,128]{2,1,0:T(8,128)(2,1)S(1)}, u32[]{:S(2)}, u32[]{:S(2)}) collective-permute-start(bf16[8,128,128]{2,1,0:T(8,128)(2,1)S(1)} %get-tuple-element.24), channel_id=1, source_target_pairs={{8,0},{9,1},{10,2},{11,3},{12,4},{13,5},{14,6},{15,7},{0,8},{1,9},... | collective-permute-start | bytes 786440 | tf_op jit(solution)/shard_map/X0D/ppermute | solution.py:193
  25.4 9.8 %collective-permute-start.9 = (bf16[8,128,128]{2,1,0:T(8,128)(2,1)S(1)}, bf16[8,128,128]{2,1,0:T(8,128)(2,1)S(1)}, u32[]{:S(2)}, u32[]{:S(2)}) collective-permute-start(bf16[8,128,128]{2,1,0:T(8,128)(2,1)S(1)} %collective-permute-done.6.refs_3_), channel_id=1, source_target_pairs={{1,0},{2,1},{3,2},{0,3},{5,4},{6,5},{7,6},{4,7},{9,8},{10,9},{11,1... | collective-permute-start | bytes 786440 | tf_op jit(solution)/shard_map/L2B/ppermute | solution.py:193
  25.5 11.3 %collective-permute-start.15 = (bf16[8,128,128]{2,1,0:T(8,128)(2,1)S(1)}, bf16[8,128,128]{2,1,0:T(8,128)(2,1)S(1)}, u32[]{:S(2)}, u32[]{:S(2)}) collective-permute-start(bf16[8,128,128]{2,1,0:T(8,128)(2,1)S(1)} %broadcast_select_fusion.6.refs_10_.refs_6_), channel_id=1, source_target_pairs={{16,0},{17,1},{18,2},{19,3},{20,4},{21,5},{22,6},{23,7},{24,8},{25... | collective-permute-start | bytes 786440 | tf_op jit(solution)/shard_map/Y1A/ppermute | solution.py:193
  31.9 8.8 %collective-permute-start.18 = (bf16[8,128,128]{2,1,0:T(8,128)(2,1)S(1)}, bf16[8,128,128]{2,1,0:T(8,128)(2,1)S(1)}, u32[]{:S(2)}, u32[]{:S(2)}) collective-permute-start(bf16[8,128,128]{2,1,0:T(8,128)(2,1)S(1)} %collective-permute-done.1.refs_4_), channel_id=1, source_target_pairs={{8,0},{9,1},{10,2},{11,3},{12,4},{13,5},{14,6},{15,7},{0,8},{1,9},... | collective-permute-start | bytes 786440 | tf_op jit(solution)/shard_map/X2A/ppermute | solution.py:193
  33.5 8.9 %collective-permute-start.10 = (bf16[8,128,128]{2,1,0:T(8,128)(2,1)S(1)}, bf16[8,128,128]{2,1,0:T(8,128)(2,1)S(1)}, u32[]{:S(2)}, u32[]{:S(2)}) collective-permute-start(bf16[8,128,128]{2,1,0:T(8,128)(2,1)S(1)} %broadcast_select_fusion.3), channel_id=1, source_target_pairs={{3,0},{0,1},{1,2},{2,3},{7,4},{4,5},{5,6},{6,7},{11,8},{8,9},{9,10... | collective-permute-start | bytes 786440 | tf_op jit(solution)/shard_map/R3A/ppermute | solution.py:193
  33.6 10.9 %collective-permute-start.4 = (bf16[8,128,128]{2,1,0:T(8,128)(2,1)S(1)}, bf16[8,128,128]{2,1,0:T(8,128)(2,1)S(1)}, u32[]{:S(2)}, u32[]{:S(2)}) collective-permute-start(bf16[8,128,128]{2,1,0:T(8,128)(2,1)S(1)} %broadcast_select_fusion.9), channel_id=1, source_target_pairs={{3,0},{0,1},{1,2},{2,3},{7,4},{4,5},{5,6},{6,7},{11,8},{8,9},{9,10... | collective-permute-start | bytes 786440 | tf_op jit(solution)/shard_map/R3B/ppermute | solution.py:193
  35.3 9.8 %collective-permute-start.20 = (bf16[8,128,128]{2,1,0:T(8,128)(2,1)S(1)}, bf16[8,128,128]{2,1,0:T(8,128)(2,1)S(1)}, u32[]{:S(2)}, u32[]{:S(2)}) collective-permute-start(bf16[8,128,128]{2,1,0:T(8,128)(2,1)S(1)} %collective-permute-done.9.refs_5_), channel_id=1, source_target_pairs={{16,0},{17,1},{18,2},{19,3},{20,4},{21,5},{22,6},{23,7},{24,8},{25... | collective-permute-start | bytes 786440 | tf_op jit(solution)/shard_map/Y2B/ppermute | solution.py:193
  36.8 12.4 %collective-permute-start.12 = (bf16[8,128,128]{2,1,0:T(8,128)(2,1)S(1)}, bf16[8,128,128]{2,1,0:T(8,128)(2,1)S(1)}, u32[]{:S(2)}, u32[]{:S(2)}) collective-permute-start(bf16[8,128,128]{2,1,0:T(8,128)(2,1)S(1)} %get-tuple-element.28.refs_6_.refs_2_), channel_id=1, source_target_pairs={{16,0},{17,1},{18,2},{19,3},{20,4},{21,5},{22,6},{23,7},{24,8},{25... | collective-permute-start | bytes 786440 | tf_op jit(solution)/shard_map/Y0A/ppermute | solution.py:193
  40.8 7.9 %collective-permute-start.17 = (bf16[8,128,128]{2,1,0:T(8,128)(2,1)S(1)}, bf16[8,128,128]{2,1,0:T(8,128)(2,1)S(1)}, u32[]{:S(2)}, u32[]{:S(2)}) collective-permute-start(bf16[8,128,128]{2,1,0:T(8,128)(2,1)S(1)} %broadcast_select_fusion.1.refs_12_.refs_8_), channel_id=1, source_target_pairs={{8,0},{9,1},{10,2},{11,3},{12,4},{13,5},{14,6},{15,7},{0,8},{1,9},... | collective-permute-start | bytes 786440 | tf_op jit(solution)/shard_map/X1B/ppermute | solution.py:193
  42.3 8.4 %collective-permute-start.13 = (bf16[8,128,128]{2,1,0:T(8,128)(2,1)S(1)}, bf16[8,128,128]{2,1,0:T(8,128)(2,1)S(1)}, u32[]{:S(2)}, u32[]{:S(2)}) collective-permute-start(bf16[8,128,128]{2,1,0:T(8,128)(2,1)S(1)} %get-tuple-element.23.refs_8_.refs_4_), channel_id=1, source_target_pairs={{8,0},{9,1},{10,2},{11,3},{12,4},{13,5},{14,6},{15,7},{0,8},{1,9},... | collective-permute-start | bytes 786440 | tf_op jit(solution)/shard_map/X0B/ppermute | solution.py:193
  44.5 9.9 %collective-permute-start.19 = (bf16[8,128,128]{2,1,0:T(8,128)(2,1)S(1)}, bf16[8,128,128]{2,1,0:T(8,128)(2,1)S(1)}, u32[]{:S(2)}, u32[]{:S(2)}) collective-permute-start(bf16[8,128,128]{2,1,0:T(8,128)(2,1)S(1)} %broadcast_select_fusion.5.refs_6_.refs_10_), channel_id=1, source_target_pairs={{16,0},{17,1},{18,2},{19,3},{20,4},{21,5},{22,6},{23,7},{24,8},{25... | collective-permute-start | bytes 786440 | tf_op jit(solution)/shard_map/Y2A/ppermute | solution.py:193
  45.0 17.0 %collective-permute-start.11 = (bf16[8,128,128]{2,1,0:T(8,128)(2,1)S(1)}, bf16[8,128,128]{2,1,0:T(8,128)(2,1)S(1)}, u32[]{:S(2)}, u32[]{:S(2)}) collective-permute-start(bf16[8,128,128]{2,1,0:T(8,128)(2,1)S(1)} %collective-permute-done.9.refs_5_), channel_id=1, source_target_pairs={{1,0},{2,1},{3,2},{0,3},{5,4},{6,5},{7,6},{4,7},{9,8},{10,9},{11,1... | collective-permute-start | bytes 786440 | tf_op jit(solution)/shard_map/L3B/ppermute | solution.py:193
  48.7 13.3 %collective-permute-start.5 = (bf16[8,128,128]{2,1,0:T(8,128)(2,1)S(1)}, bf16[8,128,128]{2,1,0:T(8,128)(2,1)S(1)}, u32[]{:S(2)}, u32[]{:S(2)}) collective-permute-start(bf16[8,128,128]{2,1,0:T(8,128)(2,1)S(1)} %collective-permute-done.1.refs_4_), channel_id=1, source_target_pairs={{1,0},{2,1},{3,2},{0,3},{5,4},{6,5},{7,6},{4,7},{9,8},{10,9},{11,1... | collective-permute-start | bytes 786440 | tf_op jit(solution)/shard_map/L3A/ppermute | solution.py:193
  49.2 6.4 %collective-permute-start.21 = (bf16[8,128,128]{2,1,0:T(8,128)(2,1)S(1)}, bf16[8,128,128]{2,1,0:T(8,128)(2,1)S(1)}, u32[]{:S(2)}, u32[]{:S(2)}) collective-permute-start(bf16[8,128,128]{2,1,0:T(8,128)(2,1)S(1)} %broadcast_select_fusion.refs_8_.refs_12_), channel_id=1, source_target_pairs={{8,0},{9,1},{10,2},{11,3},{12,4},{13,5},{14,6},{15,7},{0,8},{1,9},... | collective-permute-start | bytes 786440 | tf_op jit(solution)/shard_map/X2B/ppermute | solution.py:193
where the time goes:
time: 66.9 us; the launch traced here: 66.4 us
  starting transfers between devices  26.3 us (39%)
  waiting for transfers between devices  21 us (31%)
  Pallas kernels  14.5 us (22%)
  other arithmetic  3.49 us (5%)
  local copies, waits for them, and re-layouts  0.78 us (1%)
    ppermute x22, starting transfers between devices, moved(): return lax.ppermute(value, AXES, pairs)  26.3 us
    ppermute x22, waiting for transfers between devices, moved(): return lax.ppermute(value, AXES, pairs)  21 us
    pallas_call x3, Pallas kernels, add_terms(): pl.pallas_call(functools.partial(product_kernel, (sections, allowed, tile...  14.5 us
  transfers between devices with their start and end apart: 22, of which 8 were waited for; matrix products, arithmetic and copies ran while one was open for 3% of the time, Pallas kernels for 15%

commit v1 on v0

--- a/solution.py
+++ b/solution.py
@@ -11,13 +11,23 @@
 UNROLL = 26
 AXES = ("row", "col")
 ROWS_BY_ROWS = (((1,), (1,)), ((), ()))
-VLIM = 12
-KSPACE = pl.ANY
-AHEAD = 'AB'
-FIRST = 8
-COST = 0.25
-KS = ({0: (0, 1), 1: (0, 1), 2: (0, 1)}, {0: (2, 3), 1: (2, 3), 2: (2, 3)}, {3: (0, 1, 2, 3)})
-AFTER = {'L2B': ('Y0C',), 'L3A': ('R3B',), 'L3B': ('R3A',), 'X2A': ('X1A', 'Y1B'), 'X2B': ('X1A', 'X1B', 'Y1A', 'Y1B'), 'Y0C': ('X0A',), 'Y2A': ('X1A', 'Y1A', 'Y1B'), 'Y2B': ('X1A', 'Y1B')}
+
+STAGES = (
+    {0: (0, 1), 1: (0, 1), 2: (0, 1)},
+    {0: (2, 3), 1: (2, 3), 2: (2, 3)},
+    {3: (0, 1, 2, 3)},
+)
+
+AFTER = {
+    "L2B": ("Y0C",),
+    "L3A": ("R3B",),
+    "L3B": ("R3A",),
+    "X2A": ("X1A", "Y1B"),
+    "X2B": ("X1A", "X1B", "Y1A", "Y1B"),
+    "Y0C": ("X0A",),
+    "Y2A": ("X1A", "Y1A", "Y1B"),
+    "Y2B": ("X1A", "Y1B"),
+}
 
 
 def pair_codes(pair_slots, pair_count, slots):
@@ -158,15 +168,15 @@
     return pl.pallas_call(
         functools.partial(product_kernel, (sections, allowed, tiles, left_of, right_of, running is not None)),
         out_shape=jax.ShapeDtypeStruct((slots, side, side), jnp.float32),
-        in_specs=[pl.BlockSpec(memory_space=pltpu.SMEM)] * 2 + [pl.BlockSpec(memory_space=KSPACE)] * len(operands),
+        in_specs=[pl.BlockSpec(memory_space=pltpu.SMEM)] * 2 + [pl.BlockSpec(memory_space=pl.ANY)] * len(operands),
         out_specs=pl.BlockSpec(memory_space=pltpu.VMEM),
         scratch_shapes=[
             pltpu.VMEM((tasks, slots + 1, side, side), jnp.bfloat16),
             pltpu.VMEM((tasks, slots, side, side), jnp.bfloat16),
             pltpu.SemaphoreType.DMA((tasks + 1, 2, 2)),
         ],
-        compiler_params=pltpu.CompilerParams(vmem_limit_bytes=VLIM * 2**20),
-        cost_estimate=pl.CostEstimate(flops=int(COST * work), bytes_accessed=4 * 2**20, transcendentals=0),
+        compiler_params=pltpu.CompilerParams(vmem_limit_bytes=12 * 2**20),
+        cost_estimate=pl.CostEstimate(flops=int(0.25 * work), bytes_accessed=4 * 2**20, transcendentals=0),
     )(codes, meta, *operands)
 
 
@@ -187,9 +197,8 @@
     def moved(value, source_of):
         pairs = []
         for p, w, z in everyone:
-            if source_of(p, z) is not None:
-                q, y = source_of(p, z)
-                pairs.append((place(q, w, y), place(p, w, z)))
+            q, y = source_of(p, z)
+            pairs.append((place(q, w, y), place(p, w, z)))
         return lax.ppermute(value, AXES, pairs)
 
     filtered = jnp.where(x_live[0, 0][:, None, None] != 0, x_blocks[0, 0], jnp.zeros((), x_blocks.dtype))
@@ -211,32 +220,7 @@
     next_y = panel // 2 == (col + 1) % SECTIONS // 2
     shift = (col - panel) % SECTIONS
     meta = jnp.concatenate([entries, jnp.stack([shift, near_x.astype(jnp.int32), near_y.astype(jnp.int32), 0 * shift])])
-    done = {}
-
-    def hop(name, value, source_of):
-        waits = AFTER.get(name, ())
-        if waits:
-            value = lax.optimization_barrier((value,) + tuple(done[n] for n in waits))[0]
-        with jax.named_scope(name):
-            done[name] = moved(value, source_of)
-        return done[name]
-
-    def in_plane(name, value, flip, offset, far=False):
-        def source_of(p, z):
-            q = (z + offset) % SECTIONS
-            return (p ^ flip, z) if p ^ flip == q or (far and p ^ flip == q ^ (3 - flip)) else None
-
-        return hop(name, value, source_of)
-
-    def along(name, value, by):
-        return hop(name, value, lambda p, z: (p, (z + by) % SECTIONS))
-
-    near = {1: near_x, 2: near_y}
-
-    def stage_kernel(name, before, stage):
-        done[name] = add_terms(codes, meta, left, right, done.get(before), stage, slots, side)
-
-    made = {"a0": filtered[:FIRST], "b0": filtered[FIRST:]}
+    made = {"a0": filtered[:half], "b0": filtered[half:]}
     ops = {}
 
     def op(name, operand, source_of):
@@ -250,8 +234,7 @@
                 waits = [get(w) for w in AFTER.get(name, ())]
                 if waits:
                     value = lax.optimization_barrier((value, *waits))[0]
-                with jax.named_scope(name):
-                    made[name] = moved(value, source_of)
+                made[name] = moved(value, source_of)
             else:
                 made[name] = values[name]()
         return made[name]
@@ -275,48 +258,40 @@
             pa, pb = ("a0", "b0") if t == 1 else (f"L{t - 1}A", f"L{t - 1}B")
             op(la, functools.partial(get, pa), next_col)
             op(lb, functools.partial(get, pb), next_col)
-        if t < SECTIONS - 1 or "A" not in AHEAD:
+        if t < SECTIONS - 1:
             op(f"X{t}A", functools.partial(get, la), x_hop)
             values[f"S{t}A"] = lambda t=t, la=la: lax.select(near_x, get(la), get(f"X{t}A"))
             op(f"Y{t}A", functools.partial(get, f"S{t}A"), y_hop)
-        if t < SECTIONS - 1 or "B" not in AHEAD:
             op(f"Y{t}B", functools.partial(get, lb), y_hop)
             values[f"S{t}B"] = lambda t=t, lb=lb: lax.select(near_y, get(lb), get(f"Y{t}B"))
             op(f"X{t}B", functools.partial(get, f"S{t}B"), x_hop)
-    if AHEAD:
-        values["S0C"] = lambda: lax.select(near_x, get("X0A"), get("a0"))
-        values["S0D"] = lambda: lax.select(next_y, get("b0"), get("Y0B"))
-        op("Y0C", functools.partial(get, "S0C"), y_hop)
-        op("X0D", functools.partial(get, "S0D"), x_hop)
-        values["F0C"] = lambda: lax.select(next_y, get("S0C"), get("Y0C"))
-        values["F0D"] = lambda: lax.select(near_x, get("X0D"), get("S0D"))
-        op("R3A", functools.partial(get, "F0C"), last_col)
-        op("R3B", functools.partial(get, "F0D"), last_col)
+    values["S0C"] = lambda: lax.select(near_x, get("X0A"), get("a0"))
+    values["S0D"] = lambda: lax.select(next_y, get("b0"), get("Y0B"))
+    op("Y0C", functools.partial(get, "S0C"), y_hop)
+    op("X0D", functools.partial(get, "S0D"), x_hop)
+    values["F0C"] = lambda: lax.select(next_y, get("S0C"), get("Y0C"))
+    values["F0D"] = lambda: lax.select(near_x, get("X0D"), get("S0D"))
+    op("R3A", functools.partial(get, "F0C"), last_col)
+    op("R3B", functools.partial(get, "F0D"), last_col)
 
     def left_of(s):
         return [get("a0"), get("b0")] if s == 0 else [get(f"L{s}A"), get(f"L{s}B")]
 
     def right_of(t):
-        ahead = AHEAD if t == SECTIONS - 1 else ""
-        a = (0, get("R3A"), get("R3A")) if "A" in ahead else (1, get(f"S{t}A"), get(f"Y{t}A"))
-        b = (0, get("R3B"), get("R3B")) if "B" in ahead else (0, get(f"S{t}B"), get(f"X{t}B"))
-        return [a, b]
+        if t == SECTIONS - 1:
+            return [(0, get("R3A"), get("R3A")), (0, get("R3B"), get("R3B"))]
+        return [(1, get(f"S{t}A"), get(f"Y{t}A")), (0, get(f"S{t}B"), get(f"X{t}B"))]
 
     def kernel_stage(k):
-        stage = KS[k]
+        stage = STAGES[k]
         tiles = sorted({t for some in stage.values() for t in some})
         left, right = {s: left_of(s) for s in stage}, {t: right_of(t) for t in tiles}
         running = get(f"K{k - 1}") if k else None
-        waits = [get(w) for w in AFTER.get(f"K{k}", ())]
-        c = codes
-        if waits:
-            c = lax.optimization_barrier((codes, *waits))[0]
-        return add_terms(c, meta, left, right, running, stage, slots, side)
-
-    for k in range(len(KS)):
+        return add_terms(codes, meta, left, right, running, stage, slots, side)
+
+    for k in range(len(STAGES)):
         values[f"K{k}"] = functools.partial(kernel_stage, k)
-    done["K3"] = get(f"K{len(KS) - 1}")
-    return done["K3"][None, None]
+    return get(f"K{len(STAGES) - 1}")[None, None]
 
 
 def solution(mesh):

time: 66.9 us -> 66 us (0.987)
  the two profiles are of different devices: /device:TPU:2 before, /device:TPU:0 now
where the time goes in v1:
time: 66 us; the launch traced here: 65.1 us
  starting transfers between devices  26.4 us (40%)
  waiting for transfers between devices  23.5 us (36%)
  Pallas kernels  10.6 us (16%)
  other arithmetic  3.49 us (5%)
  local copies, waits for them, and re-layouts  0.78 us (1%)
    ppermute x22, starting transfers between devices, moved(): return lax.ppermute(value, AXES, pairs)  26.4 us
    ppermute x22, waiting for transfers between devices, moved(): return lax.ppermute(value, AXES, pairs)  23.5 us
    pallas_call x3, Pallas kernels, add_terms(): pl.pallas_call(functools.partial(product_kernel, (sections, allowed, tile...  10.6 us
  transfers between devices with their start and end apart: 22, of which 10 were waited for; matrix products, arithmetic and copies ran while one was open for 3% of the time, Pallas kernels for 10%

profile of v1, /device:TPU:0, one launch (start us, length us, event | category | flops | bytes accessed | tf_op | source)
XLA Modules:
  0.0 65.1 jit_solution(17411481121257651479)
XLA Ops:
  0.0 0.7 %compare_bitcast_fusion = pred[16]{0:T(512)(128)(4,1)S(1)} fusion(s32[1,1,16]{2,1,0:T(1,128)} %param.5), kind=kLoop, calls=%fused_computation.45 | loop fusion | flops 16 | bytes 80 | tf_op jit(solution)/shard_map/ne | solution.py:204
  0.7 1.1 %bitcast_select_fusion = bf16[16,128,128]{2,1,0:T(8,128)(2,1)S(1)} fusion(bf16[1,1,16,128,128]{4,3,2,1,0:T(8,128)(2,1)} %param.4, pred[16]{0:T(512)(128)(4,1)S(1)} %compare_bitcast_fusion), kind=kLoop, calls=%fused_computation.1 | loop fusion | flops 262144 | bytes 1048592 | tf_op jit(solution)/shard_map/jit(_where)/select_n | solution.py:204
  1.9 3.0 %collective-permute-start.2 = (bf16[8,128,128]{2,1,0:T(8,128)(2,1)S(1)}, bf16[8,128,128]{2,1,0:T(8,128)(2,1)S(1)}, u32[]{:S(2)}, u32[]{:S(2)}) collective-permute-start(bf16[8,128,128]{2,1,0:T(8,128)(2,1)S(1)} %get-tuple-element.29.refs_1_), channel_id=1, source_target_pairs={{16,0},{17,1},{18,2},{19,3},{20,4},{21,5},{22,6},{23,7},{24,8},{25... | collective-permute-start | bytes 786440 | tf_op jit(solution)/shard_map/ppermute | solution.py:202
  4.9 3.6 %collective-permute-start.6 = (bf16[8,128,128]{2,1,0:T(8,128)(2,1)S(1)}, bf16[8,128,128]{2,1,0:T(8,128)(2,1)S(1)}, u32[]{:S(2)}, u32[]{:S(2)}) collective-permute-start(bf16[8,128,128]{2,1,0:T(8,128)(2,1)S(1)} %get-tuple-element.29.refs_1_), channel_id=1, source_target_pairs={{1,0},{2,1},{3,2},{0,3},{5,4},{6,5},{7,6},{4,7},{9,8},{10,9},{11,1... | collective-permute-start | bytes 786440 | tf_op jit(solution)/shard_map/ppermute | solution.py:202
  8.5 1.5 %collective-permute-start.7 = (bf16[8,128,128]{2,1,0:T(8,128)(2,1)S(1)}, bf16[8,128,128]{2,1,0:T(8,128)(2,1)S(1)}, u32[]{:S(2)}, u32[]{:S(2)}) collective-permute-start(bf16[8,128,128]{2,1,0:T(8,128)(2,1)S(1)} %get-tuple-element.30.refs_0_), channel_id=1, source_target_pairs={{8,0},{9,1},{10,2},{11,3},{12,4},{13,5},{14,6},{15,7},{0,8},{1,9},... | collective-permute-start | bytes 786440 | tf_op jit(solution)/shard_map/ppermute | solution.py:202
  10.5 0.6 copy-done.1
  12.2 3.8 %collective-permute-done.7 = bf16[8,128,128]{2,1,0:T(8,128)(2,1)S(1)} collective-permute-done((bf16[8,128,128]{2,1,0:T(8,128)(2,1)S(1)}, bf16[8,128,128]{2,1,0:T(8,128)(2,1)S(1)}, u32[]{:S(2)}, u32[]{:S(2)}) %collective-permute-start.7) | collective-permute-done | bytes 262176 | tf_op jit(solution)/shard_map/ppermute | solution.py:202
  16.1 0.6 collective-permute-start.8
  16.6 2.8 %collective-permute-done.refs_2_ = bf16[8,128,128]{2,1,0:T(8,128)(2,1)S(1)} collective-permute-done((bf16[8,128,128]{2,1,0:T(8,128)(2,1)S(1)}, bf16[8,128,128]{2,1,0:T(8,128)(2,1)S(1)}, u32[]{:S(2)}, u32[]{:S(2)}) %collective-permute-start) | collective-permute-done | bytes 262176 | tf_op jit(solution)/shard_map/ppermute | solution.py:202
  19.4 1.5 %collective-permute-start.14 = (bf16[8,128,128]{2,1,0:T(8,128)(2,1)S(1)}, bf16[8,128,128]{2,1,0:T(8,128)(2,1)S(1)}, u32[]{:S(2)}, u32[]{:S(2)}) collective-permute-start(bf16[8,128,128]{2,1,0:T(8,128)(2,1)S(1)} %collective-permute-done.refs_2_), channel_id=1, source_target_pairs={{8,0},{9,1},{10,2},{11,3},{12,4},{13,5},{14,6},{15,7},{0,8},{1,9},... | collective-permute-start | bytes 786440 | tf_op jit(solution)/shard_map/ppermute | solution.py:202
  20.9 4.3 %collective-permute-start.1 = (bf16[8,128,128]{2,1,0:T(8,128)(2,1)S(1)}, bf16[8,128,128]{2,1,0:T(8,128)(2,1)S(1)}, u32[]{:S(2)}, u32[]{:S(2)}) collective-permute-start(bf16[8,128,128]{2,1,0:T(8,128)(2,1)S(1)} %collective-permute-done.refs_2_), channel_id=1, source_target_pairs={{1,0},{2,1},{3,2},{0,3},{5,4},{6,5},{7,6},{4,7},{9,8},{10,9},{11,1... | collective-permute-start | bytes 786440 | tf_op jit(solution)/shard_map/ppermute | solution.py:202
  27.0 1.6 %collective-permute-start.15 = (bf16[8,128,128]{2,1,0:T(8,128)(2,1)S(1)}, bf16[8,128,128]{2,1,0:T(8,128)(2,1)S(1)}, u32[]{:S(2)}, u32[]{:S(2)}) collective-permute-start(bf16[8,128,128]{2,1,0:T(8,128)(2,1)S(1)} %broadcast_select_fusion.6.refs_10_.refs_6_), channel_id=1, source_target_pairs={{16,0},{17,1},{18,2},{19,3},{20,4},{21,5},{22,6},{23,7},{24,8},{25... | collective-permute-start | bytes 786440 | tf_op jit(solution)/shard_map/ppermute | solution.py:202
  28.6 5.8 %collective-permute-done.16 = bf16[8,128,128]{2,1,0:T(8,128)(2,1)S(1)} collective-permute-done((bf16[8,128,128]{2,1,0:T(8,128)(2,1)S(1)}, bf16[8,128,128]{2,1,0:T(8,128)(2,1)S(1)}, u32[]{:S(2)}, u32[]{:S(2)}) %collective-permute-start.16) | collective-permute-done | bytes 262176 | tf_op jit(solution)/shard_map/ppermute | solution.py:202
  35.1 2.6 %collective-permute-done.9.refs_5_ = bf16[8,128,128]{2,1,0:T(8,128)(2,1)S(1)} collective-permute-done((bf16[8,128,128]{2,1,0:T(8,128)(2,1)S(1)}, bf16[8,128,128]{2,1,0:T(8,128)(2,1)S(1)}, u32[]{:S(2)}, u32[]{:S(2)}) %collective-permute-start.9) | collective-permute-done | bytes 262176 | tf_op jit(solution)/shard_map/ppermute | solution.py:202
  38.2 1.0 %collective-permute-done.15.refs_11_.refs_7_ = bf16[8,128,128]{2,1,0:T(8,128)(2,1)S(1)} collective-permute-done((bf16[8,128,128]{2,1,0:T(8,128)(2,1)S(1)}, bf16[8,128,128]{2,1,0:T(8,128)(2,1)S(1)}, u32[]{:S(2)}, u32[]{:S(2)}) %collective-permute-start.15) | collective-permute-done | bytes 262176 | tf_op jit(solution)/shard_map/ppermute | solution.py:202
  39.2 0.6 collective-permute-start.12
  39.8 3.4 %collective-permute-done.18 = bf16[8,128,128]{2,1,0:T(8,128)(2,1)S(1)} collective-permute-done((bf16[8,128,128]{2,1,0:T(8,128)(2,1)S(1)}, bf16[8,128,128]{2,1,0:T(8,128)(2,1)S(1)}, u32[]{:S(2)}, u32[]{:S(2)}) %collective-permute-start.18) | collective-permute-done | bytes 262176 | tf_op jit(solution)/shard_map/ppermute | solution.py:202
  44.1 1.2 %collective-permute-start.13 = (bf16[8,128,128]{2,1,0:T(8,128)(2,1)S(1)}, bf16[8,128,128]{2,1,0:T(8,128)(2,1)S(1)}, u32[]{:S(2)}, u32[]{:S(2)}) collective-permute-start(bf16[8,128,128]{2,1,0:T(8,128)(2,1)S(1)} %get-tuple-element.23.refs_8_.refs_4_), channel_id=1, source_target_pairs={{8,0},{9,1},{10,2},{11,3},{12,4},{13,5},{14,6},{15,7},{0,8},{1,9},... | collective-permute-start | bytes 786440 | tf_op jit(solution)/shard_map/ppermute | solution.py:202
  45.3 1.6 %collective-permute-done.4.refs_11_.refs_15_ = bf16[8,128,128]{2,1,0:T(8,128)(2,1)S(1)} collective-permute-done((bf16[8,128,128]{2,1,0:T(8,128)(2,1)S(1)}, bf16[8,128,128]{2,1,0:T(8,128)(2,1)S(1)}, u32[]{:S(2)}, u32[]{:S(2)}) %collective-permute-start.4) | collective-permute-done | bytes 262176 | tf_op jit(solution)/shard_map/ppermute | solution.py:202
  47.4 3.6 %collective-permute-start.11 = (bf16[8,128,128]{2,1,0:T(8,128)(2,1)S(1)}, bf16[8,128,128]{2,1,0:T(8,128)(2,1)S(1)}, u32[]{:S(2)}, u32[]{:S(2)}) collective-permute-start(bf16[8,128,128]{2,1,0:T(8,128)(2,1)S(1)} %collective-permute-done.9.refs_5_), channel_id=1, source_target_pairs={{1,0},{2,1},{3,2},{0,3},{5,4},{6,5},{7,6},{4,7},{9,8},{10,9},{11,1... | collective-permute-start | bytes 786440 | tf_op jit(solution)/shard_map/ppermute | solution.py:202
  52.4 3.8 %shard_map.46.refs_12_ = f32[16,128,128]{2,1,0:T(8,128)S(1)} custom-call(s32[4,104]{1,0:T(4,128)S(1)} %broadcast_add_fusion.codes, s32[8]{0:T(128)S(1)} %concatenate.3.meta, bf16[8,128,128]{2,1,0:T(8,128)(2,1)S(1)} %get-tuple-element.30.refs_0_, bf16[8,128,128]{2,1,0:T(8,128)(2,1)S(1)} %get-tuple-element.29.refs_1_, ...), custom_call_target="tpu_custom_call" | custom-call | flops 603979776 | bytes 4194304 | tf_op jit(solution)/shard_map/pallas_call | solution.py:168
  56.2 2.1 %collective-permute-done.21.refs_9_.refs_13_ = bf16[8,128,128]{2,1,0:T(8,128)(2,1)S(1)} collective-permute-done((bf16[8,128,128]{2,1,0:T(8,128)(2,1)S(1)}, bf16[8,128,128]{2,1,0:T(8,128)(2,1)S(1)}, u32[]{:S(2)}, u32[]{:S(2)}) %collective-permute-start.21) | collective-permute-done | bytes 262176 | tf_op jit(solution)/shard_map/ppermute | solution.py:202
  58.2 3.0 %shard_map.47.refs_16_ = f32[16,128,128]{2,1,0:T(8,128)S(1)} custom-call(s32[4,104]{1,0:T(4,128)S(1)} %broadcast_add_fusion.codes, s32[8]{0:T(128)S(1)} %concatenate.3.meta, bf16[8,128,128]{2,1,0:T(8,128)(2,1)S(1)} %get-tuple-element.30.refs_0_, bf16[8,128,128]{2,1,0:T(8,128)(2,1)S(1)} %get-tuple-element.29.refs_1_, ...), custom_call_target="tpu_custom_call" | custom-call | flops 603979776 | bytes 4194304 | tf_op jit(solution)/shard_map/pallas_call | solution.py:168
  61.3 3.8 %shard_map.48 = f32[16,128,128]{2,1,0:T(8,128)} custom-call(s32[4,104]{1,0:T(4,128)S(1)} %broadcast_add_fusion.codes, s32[8]{0:T(128)S(1)} %concatenate.3.meta, bf16[8,128,128]{2,1,0:T(8,128)(2,1)S(1)} %collective-permute-done.5.refs_0_, bf16[8,128,128]{2,1,0:T(8,128)(2,1)S(1)} %collective-permute-done.11.refs_1_, ...), custom_call_target="tpu_custom_call" | custom-call | flops 201326592 | bytes 4194304 | tf_op jit(solution)/shard_map/pallas_call | solution.py:168
  (49 shorter events, 7.2 us)
Async XLA Ops:
  1.9 14.1 %collective-permute-start.2 = (bf16[8,128,128]{2,1,0:T(8,128)(2,1)S(1)}, bf16[8,128,128]{2,1,0:T(8,128)(2,1)S(1)}, u32[]{:S(2)}, u32[]{:S(2)}) collective-permute-start(bf16[8,128,128]{2,1,0:T(8,128)(2,1)S(1)} %get-tuple-element.29.refs_1_), channel_id=1, source_target_pairs={{16,0},{17,1},{18,2},{19,3},{20,4},{21,5},{22,6},{23,7},{24,8},{25... | collective-permute-start | bytes 786440 | tf_op jit(solution)/shard_map/ppermute | solution.py:202
  4.9 20.3 %collective-permute-start.6 = (bf16[8,128,128]{2,1,0:T(8,128)(2,1)S(1)}, bf16[8,128,128]{2,1,0:T(8,128)(2,1)S(1)}, u32[]{:S(2)}, u32[]{:S(2)}) collective-permute-start(bf16[8,128,128]{2,1,0:T(8,128)(2,1)S(1)} %get-tuple-element.29.refs_1_), channel_id=1, source_target_pairs={{1,0},{2,1},{3,2},{0,3},{5,4},{6,5},{7,6},{4,7},{9,8},{10,9},{11,1... | collective-permute-start | bytes 786440 | tf_op jit(solution)/shard_map/ppermute | solution.py:202
  8.5 2.0 %copy-start = (s32[1,1,4,3,192]{4,2,3,1,0:T(4,128)S(1)}, s32[1,1,4,3,192]{4,2,3,1,0:T(4,128)}, u32[]{:S(2)}) copy-start(s32[1,1,4,3,192]{4,2,3,1,0:T(4,128)} %param.6) | copy-start | bytes 27652
  8.5 7.5 %collective-permute-start.7 = (bf16[8,128,128]{2,1,0:T(8,128)(2,1)S(1)}, bf16[8,128,128]{2,1,0:T(8,128)(2,1)S(1)}, u32[]{:S(2)}, u32[]{:S(2)}) collective-permute-start(bf16[8,128,128]{2,1,0:T(8,128)(2,1)S(1)} %get-tuple-element.30.refs_0_), channel_id=1, source_target_pairs={{8,0},{9,1},{10,2},{11,3},{12,4},{13,5},{14,6},{15,7},{0,8},{1,9},... | collective-permute-start | bytes 786440 | tf_op jit(solution)/shard_map/ppermute | solution.py:202
  10.0 9.4 %collective-permute-start = (bf16[8,128,128]{2,1,0:T(8,128)(2,1)S(1)}, bf16[8,128,128]{2,1,0:T(8,128)(2,1)S(1)}, u32[]{:S(2)}, u32[]{:S(2)}) collective-permute-start(bf16[8,128,128]{2,1,0:T(8,128)(2,1)S(1)} %get-tuple-element.30.refs_0_), channel_id=1, source_target_pairs={{1,0},{2,1},{3,2},{0,3},{5,4},{6,5},{7,6},{4,7},{9,8},{10,9},{11,1... | collective-permute-start | bytes 786440 | tf_op jit(solution)/shard_map/ppermute | solution.py:202
  10.5 0.7 %copy-start.1 = (s32[1,1,4]{2,1,0:T(1,128)S(1)}, s32[1,1,4]{2,1,0:T(1,128)}, u32[]{:S(2)}) copy-start(s32[1,1,4]{2,1,0:T(1,128)} %param.7) | copy-start | bytes 52
  16.1 10.8 %collective-permute-start.8 = (bf16[8,128,128]{2,1,0:T(8,128)(2,1)S(1)}, bf16[8,128,128]{2,1,0:T(8,128)(2,1)S(1)}, u32[]{:S(2)}, u32[]{:S(2)}) collective-permute-start(bf16[8,128,128]{2,1,0:T(8,128)(2,1)S(1)} %get-tuple-element.14), channel_id=1, source_target_pairs={{16,0},{17,1},{18,2},{19,3},{20,4},{21,5},{22,6},{23,7},{24,8},{25... | collective-permute-start | bytes 786440 | tf_op jit(solution)/shard_map/ppermute | solution.py:202
  19.4 7.6 %collective-permute-start.14 = (bf16[8,128,128]{2,1,0:T(8,128)(2,1)S(1)}, bf16[8,128,128]{2,1,0:T(8,128)(2,1)S(1)}, u32[]{:S(2)}, u32[]{:S(2)}) collective-permute-start(bf16[8,128,128]{2,1,0:T(8,128)(2,1)S(1)} %collective-permute-done.refs_2_), channel_id=1, source_target_pairs={{8,0},{9,1},{10,2},{11,3},{12,4},{13,5},{14,6},{15,7},{0,8},{1,9},... | collective-permute-start | bytes 786440 | tf_op jit(solution)/shard_map/ppermute | solution.py:202
  20.9 13.4 %collective-permute-start.1 = (bf16[8,128,128]{2,1,0:T(8,128)(2,1)S(1)}, bf16[8,128,128]{2,1,0:T(8,128)(2,1)S(1)}, u32[]{:S(2)}, u32[]{:S(2)}) collective-permute-start(bf16[8,128,128]{2,1,0:T(8,128)(2,1)S(1)} %collective-permute-done.refs_2_), channel_id=1, source_target_pairs={{1,0},{2,1},{3,2},{0,3},{5,4},{6,5},{7,6},{4,7},{9,8},{10,9},{11,1... | collective-permute-start | bytes 786440 | tf_op jit(solution)/shard_map/ppermute | solution.py:202
  25.2 9.1 %collective-permute-start.16 = (bf16[8,128,128]{2,1,0:T(8,128)(2,1)S(1)}, bf16[8,128,128]{2,1,0:T(8,128)(2,1)S(1)}, u32[]{:S(2)}, u32[]{:S(2)}) collective-permute-start(bf16[8,128,128]{2,1,0:T(8,128)(2,1)S(1)} %collective-permute-done.6.refs_3_), channel_id=1, source_target_pairs={{16,0},{17,1},{18,2},{19,3},{20,4},{21,5},{22,6},{23,7},{24,8},{25... | collective-permute-start | bytes 786440 | tf_op jit(solution)/shard_map/ppermute | solution.py:202
  26.3 8.6 %collective-permute-start.3 = (bf16[8,128,128]{2,1,0:T(8,128)(2,1)S(1)}, bf16[8,128,128]{2,1,0:T(8,128)(2,1)S(1)}, u32[]{:S(2)}, u32[]{:S(2)}) collective-permute-start(bf16[8,128,128]{2,1,0:T(8,128)(2,1)S(1)} %get-tuple-element.24), channel_id=1, source_target_pairs={{8,0},{9,1},{10,2},{11,3},{12,4},{13,5},{14,6},{15,7},{0,8},{1,9},... | collective-permute-start | bytes 786440 | tf_op jit(solution)/shard_map/ppermute | solution.py:202
  26.9 10.8 %collective-permute-start.9 = (bf16[8,128,128]{2,1,0:T(8,128)(2,1)S(1)}, bf16[8,128,128]{2,1,0:T(8,128)(2,1)S(1)}, u32[]{:S(2)}, u32[]{:S(2)}) collective-permute-start(bf16[8,128,128]{2,1,0:T(8,128)(2,1)S(1)} %collective-permute-done.6.refs_3_), channel_id=1, source_target_pairs={{1,0},{2,1},{3,2},{0,3},{5,4},{6,5},{7,6},{4,7},{9,8},{10,9},{11,1... | collective-permute-start | bytes 786440 | tf_op jit(solution)/shard_map/ppermute | solution.py:202
  27.0 12.2 %collective-permute-start.15 = (bf16[8,128,128]{2,1,0:T(8,128)(2,1)S(1)}, bf16[8,128,128]{2,1,0:T(8,128)(2,1)S(1)}, u32[]{:S(2)}, u32[]{:S(2)}) collective-permute-start(bf16[8,128,128]{2,1,0:T(8,128)(2,1)S(1)} %broadcast_select_fusion.6.refs_10_.refs_6_), channel_id=1, source_target_pairs={{16,0},{17,1},{18,2},{19,3},{20,4},{21,5},{22,6},{23,7},{24,8},{25... | collective-permute-start | bytes 786440 | tf_op jit(solution)/shard_map/ppermute | solution.py:202
  34.3 8.9 %collective-permute-start.18 = (bf16[8,128,128]{2,1,0:T(8,128)(2,1)S(1)}, bf16[8,128,128]{2,1,0:T(8,128)(2,1)S(1)}, u32[]{:S(2)}, u32[]{:S(2)}) collective-permute-start(bf16[8,128,128]{2,1,0:T(8,128)(2,1)S(1)} %collective-permute-done.1.refs_4_), channel_id=1, source_target_pairs={{8,0},{9,1},{10,2},{11,3},{12,4},{13,5},{14,6},{15,7},{0,8},{1,9},... | collective-permute-start | bytes 786440 | tf_op jit(solution)/shard_map/ppermute | solution.py:202
  34.9 9.2 %collective-permute-start.10 = (bf16[8,128,128]{2,1,0:T(8,128)(2,1)S(1)}, bf16[8,128,128]{2,1,0:T(8,128)(2,1)S(1)}, u32[]{:S(2)}, u32[]{:S(2)}) collective-permute-start(bf16[8,128,128]{2,1,0:T(8,128)(2,1)S(1)} %broadcast_select_fusion.3), channel_id=1, source_target_pairs={{3,0},{0,1},{1,2},{2,3},{7,4},{4,5},{5,6},{6,7},{11,8},{8,9},{9,10... | collective-permute-start | bytes 786440 | tf_op jit(solution)/shard_map/ppermute | solution.py:202
  35.0 11.9 %collective-permute-start.4 = (bf16[8,128,128]{2,1,0:T(8,128)(2,1)S(1)}, bf16[8,128,128]{2,1,0:T(8,128)(2,1)S(1)}, u32[]{:S(2)}, u32[]{:S(2)}) collective-permute-start(bf16[8,128,128]{2,1,0:T(8,128)(2,1)S(1)} %broadcast_select_fusion.9), channel_id=1, source_target_pairs={{3,0},{0,1},{1,2},{2,3},{7,4},{4,5},{5,6},{6,7},{11,8},{8,9},{9,10... | collective-permute-start | bytes 786440 | tf_op jit(solution)/shard_map/ppermute | solution.py:202
  37.7 9.7 %collective-permute-start.20 = (bf16[8,128,128]{2,1,0:T(8,128)(2,1)S(1)}, bf16[8,128,128]{2,1,0:T(8,128)(2,1)S(1)}, u32[]{:S(2)}, u32[]{:S(2)}) collective-permute-start(bf16[8,128,128]{2,1,0:T(8,128)(2,1)S(1)} %collective-permute-done.9.refs_5_), channel_id=1, source_target_pairs={{16,0},{17,1},{18,2},{19,3},{20,4},{21,5},{22,6},{23,7},{24,8},{25... | collective-permute-start | bytes 786440 | tf_op jit(solution)/shard_map/ppermute | solution.py:202
  39.2 12.5 %collective-permute-start.12 = (bf16[8,128,128]{2,1,0:T(8,128)(2,1)S(1)}, bf16[8,128,128]{2,1,0:T(8,128)(2,1)S(1)}, u32[]{:S(2)}, u32[]{:S(2)}) collective-permute-start(bf16[8,128,128]{2,1,0:T(8,128)(2,1)S(1)} %get-tuple-element.28.refs_6_.refs_2_), channel_id=1, source_target_pairs={{16,0},{17,1},{18,2},{19,3},{20,4},{21,5},{22,6},{23,7},{24,8},{25... | collective-permute-start | bytes 786440 | tf_op jit(solution)/shard_map/ppermute | solution.py:202
  43.2 7.9 %collective-permute-start.17 = (bf16[8,128,128]{2,1,0:T(8,128)(2,1)S(1)}, bf16[8,128,128]{2,1,0:T(8,128)(2,1)S(1)}, u32[]{:S(2)}, u32[]{:S(2)}) collective-permute-start(bf16[8,128,128]{2,1,0:T(8,128)(2,1)S(1)} %broadcast_select_fusion.1.refs_12_.refs_8_), channel_id=1, source_target_pairs={{8,0},{9,1},{10,2},{11,3},{12,4},{13,5},{14,6},{15,7},{0,8},{1,9},... | collective-permute-start | bytes 786440 | tf_op jit(solution)/shard_map/ppermute | solution.py:202
  44.1 8.3 %collective-permute-start.13 = (bf16[8,128,128]{2,1,0:T(8,128)(2,1)S(1)}, bf16[8,128,128]{2,1,0:T(8,128)(2,1)S(1)}, u32[]{:S(2)}, u32[]{:S(2)}) collective-permute-start(bf16[8,128,128]{2,1,0:T(8,128)(2,1)S(1)} %get-tuple-element.23.refs_8_.refs_4_), channel_id=1, source_target_pairs={{8,0},{9,1},{10,2},{11,3},{12,4},{13,5},{14,6},{15,7},{0,8},{1,9},... | collective-permute-start | bytes 786440 | tf_op jit(solution)/shard_map/ppermute | solution.py:202
  46.9 9.2 %collective-permute-start.19 = (bf16[8,128,128]{2,1,0:T(8,128)(2,1)S(1)}, bf16[8,128,128]{2,1,0:T(8,128)(2,1)S(1)}, u32[]{:S(2)}, u32[]{:S(2)}) collective-permute-start(bf16[8,128,128]{2,1,0:T(8,128)(2,1)S(1)} %broadcast_select_fusion.5.refs_6_.refs_10_), channel_id=1, source_target_pairs={{16,0},{17,1},{18,2},{19,3},{20,4},{21,5},{22,6},{23,7},{24,8},{25... | collective-permute-start | bytes 786440 | tf_op jit(solution)/shard_map/ppermute | solution.py:202
  47.4 13.8 %collective-permute-start.11 = (bf16[8,128,128]{2,1,0:T(8,128)(2,1)S(1)}, bf16[8,128,128]{2,1,0:T(8,128)(2,1)S(1)}, u32[]{:S(2)}, u32[]{:S(2)}) collective-permute-start(bf16[8,128,128]{2,1,0:T(8,128)(2,1)S(1)} %collective-permute-done.9.refs_5_), channel_id=1, source_target_pairs={{1,0},{2,1},{3,2},{0,3},{5,4},{6,5},{7,6},{4,7},{9,8},{10,9},{11,1... | collective-permute-start | bytes 786440 | tf_op jit(solution)/shard_map/ppermute | solution.py:202
  51.1 10.2 %collective-permute-start.5 = (bf16[8,128,128]{2,1,0:T(8,128)(2,1)S(1)}, bf16[8,128,128]{2,1,0:T(8,128)(2,1)S(1)}, u32[]{:S(2)}, u32[]{:S(2)}) collective-permute-start(bf16[8,128,128]{2,1,0:T(8,128)(2,1)S(1)} %collective-permute-done.1.refs_4_), channel_id=1, source_target_pairs={{1,0},{2,1},{3,2},{0,3},{5,4},{6,5},{7,6},{4,7},{9,8},{10,9},{11,1... | collective-permute-start | bytes 786440 | tf_op jit(solution)/shard_map/ppermute | solution.py:202
  51.6 6.6 %collective-permute-start.21 = (bf16[8,128,128]{2,1,0:T(8,128)(2,1)S(1)}, bf16[8,128,128]{2,1,0:T(8,128)(2,1)S(1)}, u32[]{:S(2)}, u32[]{:S(2)}) collective-permute-start(bf16[8,128,128]{2,1,0:T(8,128)(2,1)S(1)} %broadcast_select_fusion.refs_8_.refs_12_), channel_id=1, source_target_pairs={{8,0},{9,1},{10,2},{11,3},{12,4},{13,5},{14,6},{15,7},{0,8},{1,9},... | collective-permute-start | bytes 786440 | tf_op jit(solution)/shard_map/ppermute | solution.py:202
